TPU v7x, 32 devices: a whole 2x2x4 slice. The times are simulated.
32 devices in a mesh: groups: 2 (over y), length: 4 (over z), sector: 2 (over x), pair: 2 (over core).
Axes of the slice: x: 2, y: 2, z: 4, core: 2. Of those that a mesh axis runs over, the one named last changes fastest.
Arguments:
- flag_kernels: bfloat16 [4, 8, 32, 25, 1024], P('length', ('groups', 'sector', 'pair')), parts along dimension 1, may hold values from -1.1953125 to 1.1953125
- flag_unary: bfloat16 [4, 8, 32, 8, 1024], P('length', ('groups', 'sector', 'pair')), parts along dimension 1, may hold values from -8 to 8
- flag_labels: int32 [4, 8, 32, 1024], P('length', ('groups', 'sector', 'pair')), parts along dimension 1, may hold values from 0 to 7
- flag_mask: int32 [4, 8, 32, 1024], P('length', ('groups', 'sector', 'pair')), parts along dimension 1, may hold values 0 or 1
- dest_list: int32 [4, 8, 32], P('length', ('groups', 'sector', 'pair')), parts along dimension 1, may hold values from -1 to 3, as said below
- slot_list: int32 [4, 8, 32], P('length', ('groups', 'sector', 'pair')), parts along dimension 1, may hold values from -1 to 15, as said below
- res_kernels: bfloat16 [4, 8, 8, 25, 1024], P('length', ('groups', 'sector', 'pair')), parts along dimension 1, may hold values from -1.1953125 to 1.1953125
- res_unary: bfloat16 [4, 8, 8, 8, 1024], P('length', ('groups', 'sector', 'pair')), parts along dimension 1, may hold values from -8 to 8
- res_labels: int32 [4, 8, 8, 1024], P('length', ('groups', 'sector', 'pair')), parts along dimension 1, may hold values from 0 to 7
- res_mask: int32 [4, 8, 8, 1024], P('length', ('groups', 'sector', 'pair')), parts along dimension 1, may hold values 0 or 1
Outputs:
- flag_grad: bfloat16 [4, 8, 32, 25, 1024], P('length', ('groups', 'sector', 'pair')), parts along dimension 1
- res_grad: bfloat16 [4, 8, 8, 25, 1024], P('length', ('groups', 'sector', 'pair')), parts along dimension 1
- helper_loss: float32 [4, 8, 16], P('length', ('groups', 'sector', 'pair')), parts along dimension 1
There are 2 independent parts, one for each index of `groups`. A program takes and returns all parts, laid end to end along the dimension named above; each array names one. Nothing has to cross between parts.
Inputs may be any that keep to these rules, and one draw needn't show every extreme that they name: `dest_list`: entry j of a device's list is -1 exactly when its slot j holds no flagged tile, and the -1 entries come after all others; at most 8 entries of one device name the same destination. `slot_list`: for each index along sector and pair, each pair of a destination along length and a slot 0 to 15 is named by exactly one entry of the lists of the devices along length; an entry is -1 exactly where dest_list is -1.
All inputs are finite; a program needn't handle non-finite values. No bound on the sum of `flag_mask` or of `res_mask` on one device may be relied on, other than what follows from the above.
Results may differ from a plain program's by a relative error of at most 0.001.
Values may be sent and summed in bfloat16 or wider, within the bound.
A program may use at most 64 MiB of HBM per device.

v0:
```python
import functools

import jax
import jax.numpy as jnp
from jax import lax
from jax.experimental import pallas as pl
from jax.experimental.pallas import tpu as pltpu
from jax.sharding import PartitionSpec as P

CLASSES = 8
TAPS = 25
TILE = 32
ITERS = 3
RECV = 16
STEP = 8

OFFSETS = [(a, b) for a in range(-2, 3) for b in range(-2, 3)]


def shift_all(x, lane):
    after = pltpu.roll(x, 7, 0)
    before = pltpu.roll(x, 1, 0)
    shifted = []
    for a, b in OFFSETS:
        k = a * TILE + b
        if k == 0:
            shifted.append(x)
        elif k > 0:
            shifted.append(pltpu.roll(jnp.where(lane >= k, x, after), 128 - k, 1))
        else:
            shifted.append(pltpu.roll(jnp.where(lane < 128 + k, x, before), -k, 1))
    return shifted


def shift_one(x, k, lane):
    if k == 0:
        return x
    if k > 0:
        return pltpu.roll(jnp.where(lane >= k, x, pltpu.roll(x, 7, 0)), 128 - k, 1)
    return pltpu.roll(jnp.where(lane < 128 + k, x, pltpu.roll(x, 1, 0)), -k, 1)


def total(values):
    while len(values) > 1:
        values = [sum(values[i : i + 2]) for i in range(0, len(values), 2)]
    return values[0]


def tile(j, k_ref, u_ref, tgt_ref, grad_ref, loss_ref, flat, unary, kfwd, kbwd, shf):
    lane = lax.broadcasted_iota(jnp.int32, (8, 128), 1)
    sub = lax.broadcasted_iota(jnp.int32, (8, 128), 0)
    row = sub * 4 + lane // TILE
    col = lane % TILE

    def inside(t):
        a, b = OFFSETS[t]
        return (row + a >= 0) & (row + a < TILE) & (col + b >= 0) & (col + b < TILE)

    for p in range(8):
        part = slice(128 * p, 128 * (p + 1))
        flat[pl.ds(p, TAPS, stride=8), :] = k_ref[0, 0, j, :, part].astype(jnp.float32)
        unary[pl.ds(p, CLASSES, stride=8), :] = u_ref[0, 0, j, :, part].astype(jnp.float32)
    for t in range(TAPS):
        a, b = OFFSETS[t]
        masked = jnp.where(inside(t), flat[8 * t : 8 * t + 8, :], 0.0)
        kfwd[t] = masked
        kbwd[TAPS - 1 - t] = shift_one(masked, -(a * TILE + b), lane)

    def send(field, weights, keep):
        result = []
        for c in range(CLASSES):
            moved = shift_all(field[c], lane)
            if keep is not None:
                for t in range(TAPS):
                    shf[keep, t, c] = moved[t]
            sums = [moved[t] * weights[t] for t in range(5)]
            for t in range(5, TAPS):
                sums[t % 5] = sums[t % 5] + moved[t] * weights[t]
            result.append(total(sums))
        return result

    def soft(logits):
        raised = [jnp.exp(x) for x in logits]
        summed = total(raised)
        scale = 1.0 / summed
        return [x * scale for x in raised], summed

    first = [unary[8 * c : 8 * c + 8, :] for c in range(CLASSES)]
    beliefs, _ = soft(first)
    kept = [beliefs]
    for i in range(ITERS):
        sent = send(beliefs, kfwd, i)
        logits = [unary[8 * c : 8 * c + 8, :] + sent[c] for c in range(CLASSES)]
        beliefs, summed = soft(logits)
        kept.append(beliefs)
    labels = tgt_ref[j]
    used = labels < CLASSES
    chosen = total([jnp.where(labels == c, logits[c], 0.0) for c in range(CLASSES)])
    loss_ref[j] = jnp.where(used, jnp.log(summed) - chosen, 0.0)
    slope = [
        jnp.where(used, kept[3][c] - jnp.where(labels == c, 1.0, 0.0), 0.0)
        for c in range(CLASSES)
    ]
    slopes = [None, None, slope]
    for i in (1, 0):
        back = send(slopes[i + 1], kbwd, None)
        field = kept[i + 1]
        mean = total([field[c] * back[c] for c in range(CLASSES)])
        slopes[i] = [field[c] * (back[c] - mean) for c in range(CLASSES)]
    for t in range(TAPS):
        gathered = total(
            [slopes[i][c] * shf[i, t, c] for i in range(ITERS) for c in range(CLASSES)]
        )
        flat[8 * t : 8 * t + 8, :] = jnp.where(inside(t), gathered, 0.0)
    for p in range(8):
        grad_ref[0, 0, j, :, 128 * p : 128 * (p + 1)] = flat[
            pl.ds(p, TAPS, stride=8), :
        ].astype(jnp.bfloat16)


def crf_kernel(dest_ref, k_ref, u_ref, tgt_ref, grad_ref, loss_ref, *scratch):
    base = pl.program_id(0) * STEP

    @pl.loop(0, STEP)
    def _(j):
        listed = dest_ref[base + j] >= 0

        @pl.when(listed)
        def _():
            tile(j, k_ref, u_ref, tgt_ref, grad_ref, loss_ref, *scratch)

        @pl.when(jnp.logical_not(listed))
        def _():
            grad_ref[0, 0, j] = jnp.zeros(grad_ref.shape[3:], grad_ref.dtype)
            loss_ref[j] = jnp.zeros((8, 128), jnp.float32)


def crf(listed, kernels, unary, labels, mask):
    amount, taps, pixels = kernels.shape[2:]
    big = lambda d: pl.BlockSpec((1, 1, STEP, d, pixels), lambda i, s: (0, 0, i, 0, 0))
    flat = pl.BlockSpec((STEP, 8, 128), lambda i, s: (i, 0, 0))
    target = jnp.where(mask == 1, labels, CLASSES).reshape(amount, 8, 128)
    return pl.pallas_call(
        crf_kernel,
        grid_spec=pltpu.PrefetchScalarGridSpec(
            num_scalar_prefetch=1,
            grid=(amount // STEP,),
            in_specs=[big(taps), big(CLASSES), flat],
            out_specs=[big(taps), flat],
            scratch_shapes=[
                pltpu.VMEM((TAPS * 8, 128), jnp.float32),
                pltpu.VMEM((CLASSES * 8, 128), jnp.float32),
                pltpu.VMEM((TAPS, 8, 128), jnp.float32),
                pltpu.VMEM((TAPS, 8, 128), jnp.float32),
                pltpu.VMEM((ITERS, TAPS, CLASSES, 8, 128), jnp.float32),
            ],
        ),
        out_shape=[
            jax.ShapeDtypeStruct(kernels.shape, jnp.bfloat16),
            jax.ShapeDtypeStruct((amount, 8, 128), jnp.float32),
        ],
        compiler_params=pltpu.CompilerParams(vmem_limit_bytes=24 * 1024 * 1024),
    )(listed, kernels, unary, target)


def on_device(fk, fu, fl, fm, dest, slot, rk, ru, rl, rm):
    destinations, slots = dest[0, 0], slot[0, 0]
    flag_grad, partial = crf(destinations, fk, fu, fl, fm)
    count = lax.axis_size("length")
    losses = jnp.sum(partial, axis=(1, 2)) / TILE
    place = jnp.where(destinations >= 0, destinations * RECV + slots, -1)
    table = jnp.sum(
        jnp.where(place[None, :] == jnp.arange(count * RECV)[:, None], losses[None, :], 0.0), axis=1
    )
    got = lax.all_to_all(
        table.reshape(count, RECV), "length", split_axis=0, concat_axis=0, tiled=True
    )
    res_grad, _ = crf(jnp.zeros((rk.shape[2],), jnp.int32), rk, ru, rl, rm)
    return flag_grad, res_grad, jnp.sum(got, axis=0)[None, None]


def solution(mesh):
    tile_axes = ("groups", "sector", "pair")
    spec = lambda n: P("length", tile_axes, *([None] * n))
    return jax.shard_map(
        on_device,
        mesh=mesh,
        in_specs=(spec(3), spec(3), spec(2), spec(2), spec(1), spec(1), spec(3), spec(3), spec(2), spec(2)),
        out_specs=(spec(3), spec(3), spec(1)),
        check_vma=False,
    )
```

profile of v0, /device:TPU:0, one launch (start us, length us, event | category | flops | bytes accessed | tf_op | source)
XLA Modules:
  0.0 80.7 jit_solution(2408944326716220618)
XLA Ops:
  0.6 0.0 copy-start.4
  0.6 0.0 copy-start.5
  0.7 0.0 copy-start.2
  0.7 0.0 copy-start
  0.7 2.4 %copy.22.k_ref = bf16[1,1,32,25,1024]{4,3,2,1,0:T(8,128)(2,1)S(1)} copy(bf16[1,1,32,25,1024]{4,2,3,1,0:T(8,128)(2,1)} %param.10) | data formatting | bytes 3276800 | tf_op args[0]
  3.1 0.0 copy-done.4
  3.1 0.0 copy-done.5
  3.1 0.0 copy-start.8
  3.2 0.0 copy-done.2
  3.2 0.0 copy-done
  3.2 23.6 %shard_map.121 = (bf16[1,1,32,25,1024]{4,3,2,1,0:T(8,128)(2,1)S(1)}, f32[32,8,128]{2,1,0:T(8,128)S(1)}) custom-call(s32[32]{0:T(128)S(1)} %bitcast.22, bf16[1,1,32,25,1024]{4,3,2,1,0:T(8,128)(2,1)S(1)} %copy.22.k_ref, bf16[1,1,32,8,1024]{4,3,2,1,0:T(8,128)(2,1)S(1)} %copy-done, s32[32,8,128]{2,1,0:T(8,128)S(1)} %bitcast.20), custom_call_target="tpu_custom_call" | custom-call | tf_op jit(solution)/shard_map/pallas_call | solution.py:143
  26.8 0.0 copy-start.3
  26.8 0.3 reduce_sum.27
  27.2 0.0 copy-done.8
  27.2 0.1 select_reduce_fusion
  27.3 0.7 all_to_all.6
  27.9 34.8 %all-to-all-start = ((f32[4,1,16]{2,1,0:T(1,128)}), f32[4,1,16]{2,1,0:T(1,128)S(1)}, u32[]{:S(2)}, u32[]{:S(2)}) async-start(f32[4,1,16]{2,1,0:T(1,128)} %bitcast.2), calls=%async_computation | async-start | bytes 4096 | tf_op jit(solution)/shard_map/all_to_all | solution.py:175
  62.8 2.1 %copy.25 = bf16[1,1,32,25,1024]{4,2,3,1,0:T(8,128)(2,1)} copy(bf16[1,1,32,25,1024]{4,3,2,1,0:T(8,128)(2,1)S(1)} %get-tuple-element.15) | data formatting | bytes 3276800
  64.9 0.0 copy-done.3
  64.9 0.2 copy.23.k_ref
  65.2 14.0 %shard_map.122 = (bf16[1,1,8,25,1024]{4,3,2,1,0:T(8,128)(2,1)S(1)}, f32[8,8,128]{2,1,0:T(8,128)}) custom-call(s32[8]{0:T(128)S(1)} %broadcast_1_dest_ref.2.dest_ref, bf16[1,1,8,25,1024]{4,3,2,1,0:T(8,128)(2,1)S(1)} %copy.23.k_ref, bf16[1,1,8,8,1024]{4,3,2,1,0:T(8,128)(2,1)S(1)} %copy-done.1, s32[8,8,128]{2,1,0:T(8,128)S(1)} %bitcast.21), custom_call_target="tpu_custom_call" | custom-call | tf_op jit(solution)/shard_map/pallas_call | solution.py:143
  79.2 1.0 %copy.26 = bf16[1,1,8,25,1024]{4,2,3,1,0:T(8,128)(2,1)} copy(bf16[1,1,8,25,1024]{4,3,2,1,0:T(8,128)(2,1)S(1)} %get-tuple-element.16) | data formatting | bytes 819200
  80.2 0.0 all-to-all-done
  80.2 0.5 reduce_sum.29
  (13 shorter events, 0.1 us)
Async XLA Ops:
  0.6 2.5 %copy-start.4 = (s32[1,1,32,1024]{3,2,1,0:T(8,128)S(1)}, s32[1,1,32,1024]{3,2,1,0:T(8,128)}, u32[]{:S(2)}) copy-start(s32[1,1,32,1024]{3,2,1,0:T(8,128)} %param.12) | copy-start | bytes 393220
  0.6 2.5 %copy-start.5 = (s32[1,1,32,1024]{3,2,1,0:T(8,128)S(1)}, s32[1,1,32,1024]{3,2,1,0:T(8,128)}, u32[]{:S(2)}) copy-start(s32[1,1,32,1024]{3,2,1,0:T(8,128)} %param.13) | copy-start | bytes 393220
  0.7 2.6 %copy-start.2 = (s32[1,1,32]{2,1,0:T(1,128)S(1)}, s32[1,1,32]{2,1,0:T(1,128)}, u32[]{:S(2)}) copy-start(s32[1,1,32]{2,1,0:T(1,128)} %param.14) | copy-start | bytes 388
  0.7 2.6 %copy-start = (bf16[1,1,32,8,1024]{4,3,2,1,0:T(8,128)(2,1)S(1)}, bf16[1,1,32,8,1024]{4,3,2,1,0:T(8,128)(2,1)}, u32[]{:S(2)}) copy-start(bf16[1,1,32,8,1024]{4,3,2,1,0:T(8,128)(2,1)} %u_ref.2) | copy-start | bytes 1572868
  3.1 24.0 %copy-start.8 = (s32[1,1,32]{2,1,0:T(1,128)S(1)}, s32[1,1,32]{2,1,0:T(1,128)}, u32[]{:S(2)}) copy-start(s32[1,1,32]{2,1,0:T(1,128)} %param.15) | copy-start | bytes 388
  26.8 38.0 %copy-start.3 = (bf16[1,1,8,25,1024]{4,2,3,1,0:T(8,128)(2,1)S(1)}, bf16[1,1,8,25,1024]{4,2,3,1,0:T(8,128)(2,1)}, u32[]{:S(2)}) copy-start(bf16[1,1,8,25,1024]{4,2,3,1,0:T(8,128)(2,1)} %param.16) | copy-start | bytes 1228804
  27.9 52.2 %all-to-all-start = ((f32[4,1,16]{2,1,0:T(1,128)}), f32[4,1,16]{2,1,0:T(1,128)S(1)}, u32[]{:S(2)}, u32[]{:S(2)}) async-start(f32[4,1,16]{2,1,0:T(1,128)} %bitcast.2), calls=%async_computation | async-start | bytes 4096 | tf_op jit(solution)/shard_map/all_to_all | solution.py:175
  62.7 2.4 %copy-start.6 = (s32[1,1,8,1024]{3,2,1,0:T(8,128)S(1)}, s32[1,1,8,1024]{3,2,1,0:T(8,128)}, u32[]{:S(2)}) copy-start(s32[1,1,8,1024]{3,2,1,0:T(8,128)} %param.18) | copy-start | bytes 98308
  62.7 2.4 %copy-start.7 = (s32[1,1,8,1024]{3,2,1,0:T(8,128)S(1)}, s32[1,1,8,1024]{3,2,1,0:T(8,128)}, u32[]{:S(2)}) copy-start(s32[1,1,8,1024]{3,2,1,0:T(8,128)} %param.19) | copy-start | bytes 98308
  62.7 2.4 %copy-start.1 = (bf16[1,1,8,8,1024]{4,3,2,1,0:T(8,128)(2,1)S(1)}, bf16[1,1,8,8,1024]{4,3,2,1,0:T(8,128)(2,1)}, u32[]{:S(2)}) copy-start(bf16[1,1,8,8,1024]{4,3,2,1,0:T(8,128)(2,1)} %u_ref.3) | copy-start | bytes 393220
where the time goes:
time: 80.1 us; the launch traced here: 80.7 us
  Pallas kernels  37.6 us (47%)
  starting transfers between devices  34.8 us (43%)
  local copies, waits for them, and re-layouts  6.51 us (8%)
  other arithmetic  0.98 us (1%)
  between operations  0.81 us (1%)
    pallas_call x2, Pallas kernels, crf(): pl.pallas_call(crf_kernel, grid_spec=pltpu.PrefetchScalarGridSpec(num_sca...  37.6 us
    all_to_all x1, starting transfers between devices, on_device(): lax.all_to_all(table.reshape(count, RECV), 'length', split_axis=0, concat...  34.8 us
    unnamed x24, local copies, waits for them, and re-layouts  5.84 us
  transfers between devices with their start and end apart: 1, of which 0 were waited for; matrix products, arithmetic and copies ran while one was open for 4% of the time, Pallas kernels for 17%

commit v1 on v0

v1 whole, which is shorter than its diff:
```python
import functools

import jax
import jax.numpy as jnp
from jax import lax
from jax.experimental import pallas as pl
from jax.experimental.pallas import tpu as pltpu
from jax.sharding import PartitionSpec as P

CLASSES = 8
TAPS = 25
TILE = 32
ITERS = 3
RECV = 16
STEP = 8
PAD = 8
ROWS = TILE + 2 * PAD

OFFSETS = [(a, b) for a in range(-2, 3) for b in range(-2, 3)]


def total(values):
    while len(values) > 1:
        values = [sum(values[i : i + 2]) for i in range(0, len(values), 2)]
    return values[0]


def by_block(block, values):
    return jnp.where(
        block < 2,
        jnp.where(block == 0, values[0], values[1]),
        jnp.where(block == 2, values[2], values[3]),
    )


def turn(x, amount):
    amount %= 128
    return pltpu.roll(x, amount, 1) if amount else x


def tile(j, k_ref, u_ref, tgt_ref, grad_ref, loss_ref, flat, unary, krep, fields, slopes, work):
    lane = lax.broadcasted_iota(jnp.int32, (8, 128), 1)
    block = lane // TILE
    col = lane % TILE
    valid = {b: (col + b >= 0) & (col + b < TILE) for b in (-2, -1, 1, 2)}
    parts = range(4)
    groups = range(2)

    def mask(x, b):
        return jnp.where(valid[b], x, 0.0) if b else x

    for p in range(8):
        part = slice(128 * p, 128 * (p + 1))
        flat[pl.ds(p, TAPS, stride=8), :] = k_ref[0, 0, j, :, part].astype(jnp.float32)
        unary[pl.ds(p, CLASSES, stride=8), :] = u_ref[0, 0, j, :, part].astype(jnp.float32)
    for t in range(TAPS):
        x = mask(flat[8 * t : 8 * t + 8, :], OFFSETS[t][1])
        turned = [turn(x, TILE * d) for d in range(4)]
        for q in range(4):
            krep[pl.ds(t * ROWS + PAD + q, 8, stride=4), :] = by_block(
                block, [turned[(p - q) % 4] for p in range(4)]
            )
    for g in groups:
        for q in range(4):
            work[pl.ds(g * TILE + q, 8, stride=4), :] = by_block(
                block,
                [
                    turn(unary[8 * (4 * g + p) : 8 * (4 * g + p) + 8, :], TILE * (p - q))
                    for p in range(4)
                ],
            )
    wanted = tgt_ref[j]
    turned = [turn(wanted, TILE * d) for d in range(4)]
    for q in range(4):
        work[pl.ds(2 * TILE + q, 8, stride=4), :] = by_block(
            block, [turned[(p - q) % 4] for p in range(4)]
        )
    scores = [[work[g * TILE + 8 * v : g * TILE + 8 * v + 8, :] for v in parts] for g in groups]

    def over_classes(x):
        x = x + turn(x, 64)
        return x + turn(x, 32)

    def soft(logits):
        raised = [[jnp.exp(x) for x in logits[g]] for g in groups]
        summed = [over_classes(raised[0][v] + raised[1][v]) for v in parts]
        scale = [1.0 / x for x in summed]
        return [[raised[g][v] * scale[v] for v in parts] for g in groups], summed

    kept = []
    beliefs, _ = soft(scores)
    for i in range(ITERS):
        kept.append(beliefs)
        for g in groups:
            for v in parts:
                for b in range(-2, 3):
                    fields[i, g, b + 2, PAD + 8 * v : PAD + 8 * v + 8, :] = turn(
                        beliefs[g][v], -b
                    )
        logits = [[None] * 4 for _ in groups]
        for v in parts:
            sums = [[None] * 5 for _ in groups]
            for t, (a, b) in enumerate(OFFSETS):
                base = t * ROWS + PAD + 8 * v
                weight = krep[base : base + 8, :]
                for g in groups:
                    start = PAD + 8 * v + a
                    term = weight * fields[i, g, b + 2, start : start + 8, :]
                    sums[g][a + 2] = term if b == -2 else sums[g][a + 2] + term
            for g in groups:
                logits[g][v] = scores[g][v] + total(sums[g])
        beliefs, summed = soft(logits)
    kept.append(beliefs)
    loss = jnp.zeros((8, 128), jnp.float32)
    slope = [[None] * 4 for _ in groups]
    for v in parts:
        label = work[2 * TILE + 8 * v : 2 * TILE + 8 * v + 8, :]
        used = label < float(CLASSES)
        value = jnp.where(block == 0, jnp.log(summed[v]), 0.0)
        for g in groups:
            hit = label == (block + 4 * g).astype(jnp.float32)
            value = value - jnp.where(hit, logits[g][v], 0.0)
            slope[g][v] = jnp.where(used, beliefs[g][v] - jnp.where(hit, 1.0, 0.0), 0.0)
        loss = loss + jnp.where(used, value, 0.0)
    loss_ref[j] = loss
    for i in (2, 1, 0):
        for g in groups:
            for v in parts:
                slopes[i, g, PAD + 8 * v : PAD + 8 * v + 8, :] = slope[g][v]
        if i == 0:
            break
        back = [[None] * 4 for _ in groups]
        for v in parts:
            moved = [[None] * 5 for _ in groups]
            for a in range(-2, 3):
                start = PAD + 8 * v - a
                here = [slopes[i, g, start : start + 8, :] for g in groups]
                for b in range(-2, 3):
                    base = (5 * (a + 2) + b + 2) * ROWS + start
                    weight = krep[base : base + 8, :]
                    for g in groups:
                        term = weight * here[g]
                        moved[g][b + 2] = term if a == -2 else moved[g][b + 2] + term
            for g in groups:
                back[g][v] = total([turn(moved[g][b + 2], b) for b in range(-2, 3)])
        slope = [[None] * 4 for _ in groups]
        for v in parts:
            mean = over_classes(total([kept[i][g][v] * back[g][v] for g in groups]))
            for g in groups:
                slope[g][v] = kept[i][g][v] * (back[g][v] - mean)
    for v in parts:
        here = [[slopes[i, g, PAD + 8 * v : PAD + 8 * v + 8, :] for g in groups] for i in range(ITERS)]
        for t, (a, b) in enumerate(OFFSETS):
            start = PAD + 8 * v + a
            gathered = total(
                [
                    here[i][g] * fields[i, g, b + 2, start : start + 8, :]
                    for i in range(ITERS)
                    for g in groups
                ]
            )
            base = t * ROWS + PAD + 8 * v
            krep[base : base + 8, :] = gathered
    for t in range(TAPS):
        rows = [krep[pl.ds(t * ROWS + PAD + q, 8, stride=4), :] for q in range(4)]
        found = total(
            [turn(by_block(block, [rows[(p + d) % 4] for p in range(4)]), TILE * d) for d in range(4)]
        )
        flat[8 * t : 8 * t + 8, :] = mask(found, OFFSETS[t][1])
    for p in range(8):
        grad_ref[0, 0, j, :, 128 * p : 128 * (p + 1)] = flat[
            pl.ds(p, TAPS, stride=8), :
        ].astype(jnp.bfloat16)


def crf_kernel(dest_ref, k_ref, u_ref, tgt_ref, grad_ref, loss_ref, *scratch):
    base = pl.program_id(0) * STEP

    @pl.when(base == 0)
    def _():
        for ref in scratch[2:5]:
            ref[...] = jnp.zeros(ref.shape, ref.dtype)

    @pl.loop(0, STEP)
    def _(j):
        listed = dest_ref[base + j] >= 0

        @pl.when(listed)
        def _():
            tile(j, k_ref, u_ref, tgt_ref, grad_ref, loss_ref, *scratch)

        @pl.when(jnp.logical_not(listed))
        def _():
            grad_ref[0, 0, j] = jnp.zeros(grad_ref.shape[3:], grad_ref.dtype)
            loss_ref[j] = jnp.zeros((8, 128), jnp.float32)


def crf(listed, kernels, unary, labels, mask):
    amount, taps, pixels = kernels.shape[2:]
    big = lambda d: pl.BlockSpec((1, 1, STEP, d, pixels), lambda i, s: (0, 0, i, 0, 0))
    flat = pl.BlockSpec((STEP, 8, 128), lambda i, s: (i, 0, 0))
    target = jnp.where(mask == 1, labels, CLASSES).astype(jnp.float32).reshape(amount, 8, 128)
    return pl.pallas_call(
        crf_kernel,
        grid_spec=pltpu.PrefetchScalarGridSpec(
            num_scalar_prefetch=1,
            grid=(amount // STEP,),
            in_specs=[big(taps), big(CLASSES), flat],
            out_specs=[big(taps), flat],
            scratch_shapes=[
                pltpu.VMEM((TAPS * 8, 128), jnp.float32),
                pltpu.VMEM((CLASSES * 8, 128), jnp.float32),
                pltpu.VMEM((TAPS * ROWS, 128), jnp.float32),
                pltpu.VMEM((ITERS, 2, 5, ROWS, 128), jnp.float32),
                pltpu.VMEM((ITERS, 2, ROWS, 128), jnp.float32),
                pltpu.VMEM((3 * TILE, 128), jnp.float32),
            ],
        ),
        out_shape=[
            jax.ShapeDtypeStruct(kernels.shape, jnp.bfloat16),
            jax.ShapeDtypeStruct((amount, 8, 128), jnp.float32),
        ],
        compiler_params=pltpu.CompilerParams(vmem_limit_bytes=24 * 1024 * 1024),
    )(listed, kernels, unary, target)


def on_device(fk, fu, fl, fm, dest, slot, rk, ru, rl, rm):
    destinations, slots = dest[0, 0], slot[0, 0]
    flag_grad, partial = crf(destinations, fk, fu, fl, fm)
    count = lax.axis_size("length")
    losses = jnp.sum(partial, axis=(1, 2)) / TILE
    place = jnp.where(destinations >= 0, destinations * RECV + slots, -1)
    table = jnp.sum(
        jnp.where(place[None, :] == jnp.arange(count * RECV)[:, None], losses[None, :], 0.0), axis=1
    )
    got = lax.all_to_all(
        table.reshape(count, RECV), "length", split_axis=0, concat_axis=0, tiled=True
    )
    res_grad, _ = crf(jnp.zeros((rk.shape[2],), jnp.int32), rk, ru, rl, rm)
    return flag_grad, res_grad, jnp.sum(got, axis=0)[None, None]


def solution(mesh):
    tile_axes = ("groups", "sector", "pair")
    spec = lambda n: P("length", tile_axes, *([None] * n))
    return jax.shard_map(
        on_device,
        mesh=mesh,
        in_specs=(spec(3), spec(3), spec(2), spec(2), spec(1), spec(1), spec(3), spec(3), spec(2), spec(2)),
        out_specs=(spec(3), spec(3), spec(1)),
        check_vma=False,
    )
```

time: 80.1 us -> 92.4 us (1.15); the launches traced: 80.7 us -> 91.6 us
  starting transfers between devices: 34.8 us -> 42.4 us
  Pallas kernels: 37.6 us -> 40.9 us
    all_to_all x1, starting transfers between devices: 34.8 us -> 42.4 us  [on_device(): lax.all_to_all(table.reshape(count, RECV), 'length', split_axis=0, concat...]
    pallas_call x2, Pallas kernels: 37.6 us -> 40.9 us  [crf(): pl.pallas_call(crf_kernel, grid_spec=pltpu.PrefetchScalarGridSpec(num_sca...]
  transfers between devices with their start and end apart: 1 -> 1, of which waited for: 0 -> 0; matrix products, arithmetic and copies ran while one was open for 4% -> 4% of each run, Pallas kernels for 17% -> 18%
where the time goes in v1:
time: 92.4 us; the launch traced here: 91.6 us
  starting transfers between devices  42.4 us (46%)
  Pallas kernels  40.9 us (44%)
  local copies, waits for them, and re-layouts  6.51 us (7%)
  other arithmetic  0.98 us (1%)
    all_to_all x1, starting transfers between devices, on_device(): lax.all_to_all(table.reshape(count, RECV), 'length', split_axis=0, concat...  42.4 us
    pallas_call x2, Pallas kernels, crf(): pl.pallas_call(crf_kernel, grid_spec=pltpu.PrefetchScalarGridSpec(num_sca...  40.9 us
    unnamed x24, local copies, waits for them, and re-layouts  5.84 us
  transfers between devices with their start and end apart: 1, of which 0 were waited for; matrix products, arithmetic and copies ran while one was open for 4% of the time, Pallas kernels for 18%

profile of v1, /device:TPU:0, one launch (start us, length us, event | category | flops | bytes accessed | tf_op | source)
XLA Modules:
  0.0 91.6 jit_solution(6486426961583949921)
XLA Ops:
  0.6 0.0 copy-start.4
  0.6 0.0 copy-start.5
  0.7 0.0 copy-start.2
  0.7 0.0 copy-start
  0.7 2.4 %copy.22.k_ref = bf16[1,1,32,25,1024]{4,3,2,1,0:T(8,128)(2,1)S(1)} copy(bf16[1,1,32,25,1024]{4,2,3,1,0:T(8,128)(2,1)} %param.10) | data formatting | bytes 3276800 | tf_op args[0]
  3.1 0.0 copy-done.4
  3.1 0.0 copy-done.5
  3.1 0.0 copy-start.8
  3.2 0.0 copy-done.2
  3.2 0.0 copy-done
  3.2 24.2 %shard_map.121 = (bf16[1,1,32,25,1024]{4,3,2,1,0:T(8,128)(2,1)S(1)}, f32[32,8,128]{2,1,0:T(8,128)S(1)}) custom-call(s32[32]{0:T(128)S(1)} %bitcast.22, bf16[1,1,32,25,1024]{4,3,2,1,0:T(8,128)(2,1)S(1)} %copy.22.k_ref, bf16[1,1,32,8,1024]{4,3,2,1,0:T(8,128)(2,1)S(1)} %copy-done, f32[32,8,128]{2,1,0:T(8,128)S(1)} %bitcast.20), custom_call_target="tpu_custom_call" | custom-call | tf_op jit(solution)/shard_map/pallas_call | solution.py:203
  27.5 0.0 copy-start.3
  27.5 0.3 reduce_sum.27
  27.8 0.0 copy-done.8
  27.8 0.1 select_reduce_fusion
  27.9 0.7 all_to_all.6
  28.6 42.4 %all-to-all-start = ((f32[4,1,16]{2,1,0:T(1,128)}), f32[4,1,16]{2,1,0:T(1,128)S(1)}, u32[]{:S(2)}, u32[]{:S(2)}) async-start(f32[4,1,16]{2,1,0:T(1,128)} %bitcast.2), calls=%async_computation | async-start | bytes 4096 | tf_op jit(solution)/shard_map/all_to_all | solution.py:236
  71.0 2.1 %copy.25 = bf16[1,1,32,25,1024]{4,2,3,1,0:T(8,128)(2,1)} copy(bf16[1,1,32,25,1024]{4,3,2,1,0:T(8,128)(2,1)S(1)} %get-tuple-element.15) | data formatting | bytes 3276800
  73.1 0.0 copy-done.3
  73.1 0.2 copy.23.k_ref
  73.4 16.7 %shard_map.122 = (bf16[1,1,8,25,1024]{4,3,2,1,0:T(8,128)(2,1)S(1)}, f32[8,8,128]{2,1,0:T(8,128)}) custom-call(s32[8]{0:T(128)S(1)} %broadcast_1_dest_ref.2.dest_ref, bf16[1,1,8,25,1024]{4,3,2,1,0:T(8,128)(2,1)S(1)} %copy.23.k_ref, bf16[1,1,8,8,1024]{4,3,2,1,0:T(8,128)(2,1)S(1)} %copy-done.1, f32[8,8,128]{2,1,0:T(8,128)S(1)} %bitcast.21), custom_call_target="tpu_custom_call" | custom-call | tf_op jit(solution)/shard_map/pallas_call | solution.py:203
  90.1 1.0 %copy.26 = bf16[1,1,8,25,1024]{4,2,3,1,0:T(8,128)(2,1)} copy(bf16[1,1,8,25,1024]{4,3,2,1,0:T(8,128)(2,1)S(1)} %get-tuple-element.16) | data formatting | bytes 819200
  91.1 0.0 all-to-all-done
  91.1 0.5 reduce_sum.29
  (13 shorter events, 0.1 us)
Async XLA Ops:
  0.6 2.5 %copy-start.4 = (s32[1,1,32,1024]{3,2,1,0:T(8,128)S(1)}, s32[1,1,32,1024]{3,2,1,0:T(8,128)}, u32[]{:S(2)}) copy-start(s32[1,1,32,1024]{3,2,1,0:T(8,128)} %param.12) | copy-start | bytes 393220
  0.6 2.5 %copy-start.5 = (s32[1,1,32,1024]{3,2,1,0:T(8,128)S(1)}, s32[1,1,32,1024]{3,2,1,0:T(8,128)}, u32[]{:S(2)}) copy-start(s32[1,1,32,1024]{3,2,1,0:T(8,128)} %param.13) | copy-start | bytes 393220
  0.7 2.6 %copy-start.2 = (s32[1,1,32]{2,1,0:T(1,128)S(1)}, s32[1,1,32]{2,1,0:T(1,128)}, u32[]{:S(2)}) copy-start(s32[1,1,32]{2,1,0:T(1,128)} %param.14) | copy-start | bytes 388
  0.7 2.6 %copy-start = (bf16[1,1,32,8,1024]{4,3,2,1,0:T(8,128)(2,1)S(1)}, bf16[1,1,32,8,1024]{4,3,2,1,0:T(8,128)(2,1)}, u32[]{:S(2)}) copy-start(bf16[1,1,32,8,1024]{4,3,2,1,0:T(8,128)(2,1)} %u_ref.2) | copy-start | bytes 1572868
  3.1 24.7 %copy-start.8 = (s32[1,1,32]{2,1,0:T(1,128)S(1)}, s32[1,1,32]{2,1,0:T(1,128)}, u32[]{:S(2)}) copy-start(s32[1,1,32]{2,1,0:T(1,128)} %param.15) | copy-start | bytes 388
  27.5 45.6 %copy-start.3 = (bf16[1,1,8,25,1024]{4,2,3,1,0:T(8,128)(2,1)S(1)}, bf16[1,1,8,25,1024]{4,2,3,1,0:T(8,128)(2,1)}, u32[]{:S(2)}) copy-start(bf16[1,1,8,25,1024]{4,2,3,1,0:T(8,128)(2,1)} %param.16) | copy-start | bytes 1228804
  28.6 62.5 %all-to-all-start = ((f32[4,1,16]{2,1,0:T(1,128)}), f32[4,1,16]{2,1,0:T(1,128)S(1)}, u32[]{:S(2)}, u32[]{:S(2)}) async-start(f32[4,1,16]{2,1,0:T(1,128)} %bitcast.2), calls=%async_computation | async-start | bytes 4096 | tf_op jit(solution)/shard_map/all_to_all | solution.py:236
  71.0 2.4 %copy-start.6 = (s32[1,1,8,1024]{3,2,1,0:T(8,128)S(1)}, s32[1,1,8,1024]{3,2,1,0:T(8,128)}, u32[]{:S(2)}) copy-start(s32[1,1,8,1024]{3,2,1,0:T(8,128)} %param.18) | copy-start | bytes 98308
  71.0 2.4 %copy-start.7 = (s32[1,1,8,1024]{3,2,1,0:T(8,128)S(1)}, s32[1,1,8,1024]{3,2,1,0:T(8,128)}, u32[]{:S(2)}) copy-start(s32[1,1,8,1024]{3,2,1,0:T(8,128)} %param.19) | copy-start | bytes 98308
  71.0 2.4 %copy-start.1 = (bf16[1,1,8,8,1024]{4,3,2,1,0:T(8,128)(2,1)S(1)}, bf16[1,1,8,8,1024]{4,3,2,1,0:T(8,128)(2,1)}, u32[]{:S(2)}) copy-start(bf16[1,1,8,8,1024]{4,3,2,1,0:T(8,128)(2,1)} %u_ref.3) | copy-start | bytes 393220

commit v2 on v0

--- a/solution.py
+++ b/solution.py
@@ -12,7 +12,7 @@
 TILE = 32
 ITERS = 3
 RECV = 16
-STEP = 8
+BATCH = 16
 
 OFFSETS = [(a, b) for a in range(-2, 3) for b in range(-2, 3)]
 
@@ -46,7 +46,7 @@
     return values[0]
 
 
-def tile(j, k_ref, u_ref, tgt_ref, grad_ref, loss_ref, flat, unary, kfwd, kbwd, shf):
+def tile(j, tgt_ref, loss_ref, flat, unary, kfwd, kbwd, shf):
     lane = lax.broadcasted_iota(jnp.int32, (8, 128), 1)
     sub = lax.broadcasted_iota(jnp.int32, (8, 128), 0)
     row = sub * 4 + lane // TILE
@@ -56,13 +56,9 @@
         a, b = OFFSETS[t]
         return (row + a >= 0) & (row + a < TILE) & (col + b >= 0) & (col + b < TILE)
 
-    for p in range(8):
-        part = slice(128 * p, 128 * (p + 1))
-        flat[pl.ds(p, TAPS, stride=8), :] = k_ref[0, 0, j, :, part].astype(jnp.float32)
-        unary[pl.ds(p, CLASSES, stride=8), :] = u_ref[0, 0, j, :, part].astype(jnp.float32)
     for t in range(TAPS):
         a, b = OFFSETS[t]
-        masked = jnp.where(inside(t), flat[8 * t : 8 * t + 8, :], 0.0)
+        masked = jnp.where(inside(t), flat[pl.ds(pl.multiple_of(j * (TAPS * 8) + 8 * t, 8), 8), :], 0.0)
         kfwd[t] = masked
         kbwd[TAPS - 1 - t] = shift_one(masked, -(a * TILE + b), lane)
 
@@ -85,12 +81,12 @@
         scale = 1.0 / summed
         return [x * scale for x in raised], summed
 
-    first = [unary[8 * c : 8 * c + 8, :] for c in range(CLASSES)]
+    first = [unary[pl.ds(pl.multiple_of(j * (CLASSES * 8) + 8 * c, 8), 8), :] for c in range(CLASSES)]
     beliefs, _ = soft(first)
     kept = [beliefs]
     for i in range(ITERS):
         sent = send(beliefs, kfwd, i)
-        logits = [unary[8 * c : 8 * c + 8, :] + sent[c] for c in range(CLASSES)]
+        logits = [unary[pl.ds(pl.multiple_of(j * (CLASSES * 8) + 8 * c, 8), 8), :] + sent[c] for c in range(CLASSES)]
         beliefs, summed = soft(logits)
         kept.append(beliefs)
     labels = tgt_ref[j]
@@ -111,45 +107,66 @@
         gathered = total(
             [slopes[i][c] * shf[i, t, c] for i in range(ITERS) for c in range(CLASSES)]
         )
-        flat[8 * t : 8 * t + 8, :] = jnp.where(inside(t), gathered, 0.0)
+        flat[pl.ds(pl.multiple_of(j * (TAPS * 8) + 8 * t, 8), 8), :] = jnp.where(inside(t), gathered, 0.0)
+
+
+def crf_kernel(dest_ref, k_ref, u_ref, tgt_ref, grad_ref, loss_ref, *scratch):
+    step = tgt_ref.shape[0]
+    base = pl.program_id(0) * step
+    flat, unary = scratch[:2]
     for p in range(8):
-        grad_ref[0, 0, j, :, 128 * p : 128 * (p + 1)] = flat[
-            pl.ds(p, TAPS, stride=8), :
-        ].astype(jnp.bfloat16)
-
-
-def crf_kernel(dest_ref, k_ref, u_ref, tgt_ref, grad_ref, loss_ref, *scratch):
-    base = pl.program_id(0) * STEP
-
-    @pl.loop(0, STEP)
+        part = slice(128 * p, 128 * (p + 1))
+        for t in range(TAPS):
+            flat[pl.ds(8 * t + p, step, stride=8 * TAPS), :] = k_ref[0, 0, t, :, part].astype(
+                jnp.float32
+            )
+
+    @pl.loop(0, step)
     def _(j):
         listed = dest_ref[base + j] >= 0
 
         @pl.when(listed)
         def _():
-            tile(j, k_ref, u_ref, tgt_ref, grad_ref, loss_ref, *scratch)
+            for p in range(8):
+                part = slice(128 * p, 128 * (p + 1))
+                start = j * (CLASSES * 8) + p
+                unary[pl.ds(start, CLASSES, stride=8), :] = u_ref[0, 0, j, :, part].astype(
+                    jnp.float32
+                )
+            tile(j, tgt_ref, loss_ref, *scratch)
 
         @pl.when(jnp.logical_not(listed))
         def _():
-            grad_ref[0, 0, j] = jnp.zeros(grad_ref.shape[3:], grad_ref.dtype)
+            start = pl.multiple_of(j * (TAPS * 8), 8)
+            flat[pl.ds(start, TAPS * 8), :] = jnp.zeros((TAPS * 8, 128), jnp.float32)
             loss_ref[j] = jnp.zeros((8, 128), jnp.float32)
+
+    for p in range(8):
+        part = slice(128 * p, 128 * (p + 1))
+        for t in range(TAPS):
+            grad_ref[0, 0, t, :, part] = flat[
+                pl.ds(8 * t + p, step, stride=8 * TAPS), :
+            ].astype(jnp.bfloat16)
 
 
 def crf(listed, kernels, unary, labels, mask):
     amount, taps, pixels = kernels.shape[2:]
-    big = lambda d: pl.BlockSpec((1, 1, STEP, d, pixels), lambda i, s: (0, 0, i, 0, 0))
-    flat = pl.BlockSpec((STEP, 8, 128), lambda i, s: (i, 0, 0))
+    step = min(BATCH, amount)
+    kernels = jnp.swapaxes(kernels, 2, 3)
+    taps_first = pl.BlockSpec((1, 1, taps, step, pixels), lambda i, s: (0, 0, 0, i, 0))
+    scores = pl.BlockSpec((1, 1, step, CLASSES, pixels), lambda i, s: (0, 0, i, 0, 0))
+    fields = pl.BlockSpec((step, 8, 128), lambda i, s: (i, 0, 0))
     target = jnp.where(mask == 1, labels, CLASSES).reshape(amount, 8, 128)
-    return pl.pallas_call(
+    grad, loss = pl.pallas_call(
         crf_kernel,
         grid_spec=pltpu.PrefetchScalarGridSpec(
             num_scalar_prefetch=1,
-            grid=(amount // STEP,),
-            in_specs=[big(taps), big(CLASSES), flat],
-            out_specs=[big(taps), flat],
+            grid=(amount // step,),
+            in_specs=[taps_first, scores, fields],
+            out_specs=[taps_first, fields],
             scratch_shapes=[
-                pltpu.VMEM((TAPS * 8, 128), jnp.float32),
-                pltpu.VMEM((CLASSES * 8, 128), jnp.float32),
+                pltpu.VMEM((step * TAPS * 8, 128), jnp.float32),
+                pltpu.VMEM((step * CLASSES * 8, 128), jnp.float32),
                 pltpu.VMEM((TAPS, 8, 128), jnp.float32),
                 pltpu.VMEM((TAPS, 8, 128), jnp.float32),
                 pltpu.VMEM((ITERS, TAPS, CLASSES, 8, 128), jnp.float32),
@@ -159,8 +176,9 @@
             jax.ShapeDtypeStruct(kernels.shape, jnp.bfloat16),
             jax.ShapeDtypeStruct((amount, 8, 128), jnp.float32),
         ],
-        compiler_params=pltpu.CompilerParams(vmem_limit_bytes=24 * 1024 * 1024),
+        compiler_params=pltpu.CompilerParams(vmem_limit_bytes=32 * 1024 * 1024),
     )(listed, kernels, unary, target)
+    return jnp.swapaxes(grad, 2, 3), loss
 
 
 def on_device(fk, fu, fl, fm, dest, slot, rk, ru, rl, rm):

time: 80.1 us -> 79.2 us (0.989)
  the two profiles are of different devices: /device:TPU:0 before, /device:TPU:15 now
where the time goes in v2:
time: 79.2 us; the launch traced here: 79 us
  starting transfers between devices  41.8 us (53%)
  Pallas kernels  30.6 us (39%)
  local copies, waits for them, and re-layouts  3.87 us (5%)
  other arithmetic  2 us (3%)
    all_to_all x1, starting transfers between devices, on_device(): lax.all_to_all(table.reshape(count, RECV), 'length', split_axis=0, concat...  41.8 us
    pallas_call x2, Pallas kernels, crf(): pl.pallas_call(crf_kernel, grid_spec=pltpu.PrefetchScalarGridSpec(num_sca...  30.6 us
    unnamed x20, local copies, waits for them, and re-layouts  3.18 us
  transfers between devices with their start and end apart: 1, of which 0 were waited for; matrix products, arithmetic and copies ran while one was open for 0% of the time, Pallas kernels for 18%

profile of v2, /device:TPU:15, one launch (start us, length us, event | category | flops | bytes accessed | tf_op | source)
XLA Modules:
  0.0 79.0 jit_solution(10719177473905272569)
XLA Ops:
  0.6 0.0 copy-start.5
  0.6 0.0 copy-start.8
  0.7 0.0 copy-start.6
  0.7 0.0 copy-start.7
  0.7 0.0 copy-start.2
  0.7 0.0 copy-start.3
  0.7 1.0 %select_bitcast_fusion = s32[4,8,8,128]{3,1,2,0:T(8,128)S(1)} fusion(s32[1,1,32,1024]{3,2,1,0:T(8,128)} %param.12, s32[1,1,32,1024]{3,2,1,0:T(8,128)} %param.13), kind=kLoop, calls=%fused_computation | loop fusion | flops 65536 | bytes 393216
  1.8 0.0 copy-start
  1.8 1.4 %copy-done = bf16[1,1,32,25,1024]{4,2,3,1,0:T(8,128)(2,1)S(1)} copy-done((bf16[1,1,32,25,1024]{4,2,3,1,0:T(8,128)(2,1)S(1)}, bf16[1,1,32,25,1024]{4,2,3,1,0:T(8,128)(2,1)}, u32[]{:S(2)}) %copy-start) | copy-done | bytes 1638424
  3.2 1.0 %copy-done.1 = bf16[1,1,32,8,1024]{4,3,2,1,0:T(8,128)(2,1)S(1)} copy-done((bf16[1,1,32,8,1024]{4,3,2,1,0:T(8,128)(2,1)S(1)}, bf16[1,1,32,8,1024]{4,3,2,1,0:T(8,128)(2,1)}, u32[]{:S(2)}) %copy-start.1) | copy-done | bytes 524312
  4.3 0.7 copy-done.4
  4.9 16.4 %shard_map.121 = (bf16[1,1,25,32,1024]{4,3,2,1,0:T(8,128)(2,1)}, f32[32,8,128]{2,1,0:T(8,128)S(1)}) custom-call(s32[32]{0:T(128)S(1)} %bitcast.28, bf16[1,1,25,32,1024]{4,3,2,1,0:T(8,128)(2,1)S(1)} %bitcast.24, bf16[1,1,32,8,1024]{4,3,2,1,0:T(8,128)(2,1)S(1)} %copy-done.1, s32[32,8,128]{2,1,0:T(8,128)S(1)} %bitcast.25), custom_call_target="tpu_custom_call" | custom-call | tf_op jit(solution)/shard_map/pallas_call | solution.py:160
  21.3 0.3 reduce_sum.27
  21.6 0.0 copy-done.5
  21.6 0.0 copy-done.8
  21.6 0.1 select_reduce_fusion
  21.7 0.7 all_to_all.6
  22.4 41.8 %all-to-all-start = ((f32[4,1,16]{2,1,0:T(1,128)}), f32[4,1,16]{2,1,0:T(1,128)S(1)}, u32[]{:S(2)}, u32[]{:S(2)}) async-start(f32[4,1,16]{2,1,0:T(1,128)} %bitcast.6), calls=%async_computation | async-start | bytes 4096 | tf_op jit(solution)/shard_map/all_to_all | solution.py:193
  64.2 0.0 copy-done.6
  64.2 0.0 copy-done.7
  64.2 0.0 copy-done.2
  64.3 14.2 %shard_map.122 = (bf16[1,1,25,8,1024]{4,3,2,1,0:T(8,128)(2,1)}, f32[8,8,128]{2,1,0:T(8,128)}) custom-call(s32[8]{0:T(128)S(1)} %broadcast_1_dest_ref.2.dest_ref, bf16[1,1,25,8,1024]{4,3,2,1,0:T(8,128)(2,1)S(1)} %bitcast.26, bf16[1,1,8,8,1024]{4,3,2,1,0:T(8,128)(2,1)S(1)} %copy-done.3, s32[8,8,128]{2,1,0:T(8,128)S(1)} %bitcast.27), custom_call_target="tpu_custom_call" | custom-call | tf_op jit(solution)/shard_map/pallas_call | solution.py:160
  78.4 0.0 all-to-all-done
  78.4 0.5 reduce_sum.29
  (9 shorter events, 0.1 us)
Async XLA Ops:
  0.6 21.0 %copy-start.5 = (s32[1,1,32]{2,1,0:T(1,128)S(1)}, s32[1,1,32]{2,1,0:T(1,128)}, u32[]{:S(2)}) copy-start(s32[1,1,32]{2,1,0:T(1,128)} %param.14) | copy-start | bytes 388
  0.6 21.0 %copy-start.8 = (s32[1,1,32]{2,1,0:T(1,128)S(1)}, s32[1,1,32]{2,1,0:T(1,128)}, u32[]{:S(2)}) copy-start(s32[1,1,32]{2,1,0:T(1,128)} %param.15) | copy-start | bytes 388
  0.7 63.5 %copy-start.6 = (s32[1,1,8,1024]{3,2,1,0:T(8,128)S(1)}, s32[1,1,8,1024]{3,2,1,0:T(8,128)}, u32[]{:S(2)}) copy-start(s32[1,1,8,1024]{3,2,1,0:T(8,128)} %param.18) | copy-start | bytes 98308
  0.7 63.5 %copy-start.7 = (s32[1,1,8,1024]{3,2,1,0:T(8,128)S(1)}, s32[1,1,8,1024]{3,2,1,0:T(8,128)}, u32[]{:S(2)}) copy-start(s32[1,1,8,1024]{3,2,1,0:T(8,128)} %param.19) | copy-start | bytes 98308
  0.7 63.6 %copy-start.2 = (bf16[1,1,8,25,1024]{4,2,3,1,0:T(8,128)(2,1)S(1)}, bf16[1,1,8,25,1024]{4,2,3,1,0:T(8,128)(2,1)}, u32[]{:S(2)}) copy-start(bf16[1,1,8,25,1024]{4,2,3,1,0:T(8,128)(2,1)} %param.16) | copy-start | bytes 1228804
  0.7 63.6 %copy-start.3 = (bf16[1,1,8,8,1024]{4,3,2,1,0:T(8,128)(2,1)S(1)}, bf16[1,1,8,8,1024]{4,3,2,1,0:T(8,128)(2,1)}, u32[]{:S(2)}) copy-start(bf16[1,1,8,8,1024]{4,3,2,1,0:T(8,128)(2,1)} %u_ref.3) | copy-start | bytes 393220
  1.8 1.4 %copy-start = (bf16[1,1,32,25,1024]{4,2,3,1,0:T(8,128)(2,1)S(1)}, bf16[1,1,32,25,1024]{4,2,3,1,0:T(8,128)(2,1)}, u32[]{:S(2)}) copy-start(bf16[1,1,32,25,1024]{4,2,3,1,0:T(8,128)(2,1)} %param.10) | copy-start | bytes 4915204
  3.2 1.0 %copy-start.1 = (bf16[1,1,32,8,1024]{4,3,2,1,0:T(8,128)(2,1)S(1)}, bf16[1,1,32,8,1024]{4,3,2,1,0:T(8,128)(2,1)}, u32[]{:S(2)}) copy-start(bf16[1,1,32,8,1024]{4,3,2,1,0:T(8,128)(2,1)} %u_ref.2) | copy-start | bytes 1572868
  4.3 0.7 copy-start.4
  22.4 56.0 %all-to-all-start = ((f32[4,1,16]{2,1,0:T(1,128)}), f32[4,1,16]{2,1,0:T(1,128)S(1)}, u32[]{:S(2)}, u32[]{:S(2)}) async-start(f32[4,1,16]{2,1,0:T(1,128)} %bitcast.6), calls=%async_computation | async-start | bytes 4096 | tf_op jit(solution)/shard_map/all_to_all | solution.py:193

commit v3 on v2

--- a/solution.py
+++ b/solution.py
@@ -13,6 +13,7 @@
 ITERS = 3
 RECV = 16
 BATCH = 16
+TOGETHER = 2
 
 OFFSETS = [(a, b) for a in range(-2, 3) for b in range(-2, 3)]
 
@@ -62,6 +63,8 @@
         kfwd[t] = masked
         kbwd[TAPS - 1 - t] = shift_one(masked, -(a * TILE + b), lane)
 
+    yield
+
     def send(field, weights, keep):
         result = []
         for c in range(CLASSES):
@@ -86,8 +89,10 @@
     kept = [beliefs]
     for i in range(ITERS):
         sent = send(beliefs, kfwd, i)
+        yield
         logits = [unary[pl.ds(pl.multiple_of(j * (CLASSES * 8) + 8 * c, 8), 8), :] + sent[c] for c in range(CLASSES)]
         beliefs, summed = soft(logits)
+        yield
         kept.append(beliefs)
     labels = tgt_ref[j]
     used = labels < CLASSES
@@ -100,13 +105,17 @@
     slopes = [None, None, slope]
     for i in (1, 0):
         back = send(slopes[i + 1], kbwd, None)
+        yield
         field = kept[i + 1]
         mean = total([field[c] * back[c] for c in range(CLASSES)])
         slopes[i] = [field[c] * (back[c] - mean) for c in range(CLASSES)]
+        yield
     for t in range(TAPS):
-        gathered = total(
-            [slopes[i][c] * shf[i, t, c] for i in range(ITERS) for c in range(CLASSES)]
-        )
+        chains = [slopes[0][c] * shf[0, t, c] for c in range(4)]
+        for n in range(4, ITERS * CLASSES):
+            i, c = n // CLASSES, n % CLASSES
+            chains[n % 4] = chains[n % 4] + slopes[i][c] * shf[i, t, c]
+        gathered = total(chains)
         flat[pl.ds(pl.multiple_of(j * (TAPS * 8) + 8 * t, 8), 8), :] = jnp.where(inside(t), gathered, 0.0)
 
 
@@ -121,25 +130,37 @@
                 jnp.float32
             )
 
-    @pl.loop(0, step)
-    def _(j):
-        listed = dest_ref[base + j] >= 0
-
-        @pl.when(listed)
+    def clear(j):
+        start = pl.multiple_of(j * (TAPS * 8), 8)
+        flat[pl.ds(start, TAPS * 8), :] = jnp.zeros((TAPS * 8, 128), jnp.float32)
+        loss_ref[j] = jnp.zeros((8, 128), jnp.float32)
+
+    @pl.loop(0, step // TOGETHER)
+    def _(n):
+        members = [n * TOGETHER + w for w in range(TOGETHER)]
+        listed = [dest_ref[base + j] >= 0 for j in members]
+
+        @pl.when(functools.reduce(jnp.logical_or, listed))
         def _():
-            for p in range(8):
-                part = slice(128 * p, 128 * (p + 1))
-                start = j * (CLASSES * 8) + p
-                unary[pl.ds(start, CLASSES, stride=8), :] = u_ref[0, 0, j, :, part].astype(
-                    jnp.float32
-                )
-            tile(j, tgt_ref, loss_ref, *scratch)
-
-        @pl.when(jnp.logical_not(listed))
-        def _():
-            start = pl.multiple_of(j * (TAPS * 8), 8)
-            flat[pl.ds(start, TAPS * 8), :] = jnp.zeros((TAPS * 8, 128), jnp.float32)
-            loss_ref[j] = jnp.zeros((8, 128), jnp.float32)
+            for j in members:
+                for p in range(8):
+                    part = slice(128 * p, 128 * (p + 1))
+                    start = j * (CLASSES * 8) + p
+                    unary[pl.ds(start, CLASSES, stride=8), :] = u_ref[0, 0, j, :, part].astype(
+                        jnp.float32
+                    )
+            steps = [
+                tile(j, tgt_ref, loss_ref, flat, unary, *[ref.at[w] for ref in scratch[2:]])
+                for w, j in enumerate(members)
+            ]
+            for _ in zip(*steps):
+                pass
+            for rest in steps[1:]:
+                for _ in rest:
+                    pass
+
+        for j, known in zip(members, listed):
+            pl.when(jnp.logical_not(known))(functools.partial(clear, j))
 
     for p in range(8):
         part = slice(128 * p, 128 * (p + 1))
@@ -167,9 +188,9 @@
             scratch_shapes=[
                 pltpu.VMEM((step * TAPS * 8, 128), jnp.float32),
                 pltpu.VMEM((step * CLASSES * 8, 128), jnp.float32),
-                pltpu.VMEM((TAPS, 8, 128), jnp.float32),
-                pltpu.VMEM((TAPS, 8, 128), jnp.float32),
-                pltpu.VMEM((ITERS, TAPS, CLASSES, 8, 128), jnp.float32),
+                pltpu.VMEM((TOGETHER, TAPS, 8, 128), jnp.float32),
+                pltpu.VMEM((TOGETHER, TAPS, 8, 128), jnp.float32),
+                pltpu.VMEM((TOGETHER, ITERS, TAPS, CLASSES, 8, 128), jnp.float32),
             ],
         ),
         out_shape=[

time: 79.2 us -> 68.7 us (0.87)
  the two profiles are of different devices: /device:TPU:15 before, /device:TPU:0 now
where the time goes in v3:
time: 68.7 us; the launch traced here: 68.9 us
  Pallas kernels  43.4 us (63%)
  starting transfers between devices  18.9 us (28%)
  local copies, waits for them, and re-layouts  3.87 us (6%)
  other arithmetic  2 us (3%)
  between operations  0.75 us (1%)
    pallas_call x2, Pallas kernels, crf(): pl.pallas_call(crf_kernel, grid_spec=pltpu.PrefetchScalarGridSpec(num_sca...  43.4 us
    all_to_all x1, starting transfers between devices, on_device(): lax.all_to_all(table.reshape(count, RECV), 'length', split_axis=0, concat...  18.9 us
    unnamed x20, local copies, waits for them, and re-layouts  3.18 us
  transfers between devices with their start and end apart: 1, of which 0 were waited for; matrix products, arithmetic and copies ran while one was open for 0% of the time, Pallas kernels for 17%

profile of v3, /device:TPU:0, one launch (start us, length us, event | category | flops | bytes accessed | tf_op | source)
XLA Modules:
  0.0 68.9 jit_solution(17621657274615283050)
XLA Ops:
  0.6 0.0 copy-start.5
  0.6 0.0 copy-start.8
  0.7 0.0 copy-start.6
  0.7 0.0 copy-start.7
  0.7 0.0 copy-start.2
  0.7 0.0 copy-start.3
  0.7 1.0 %select_bitcast_fusion = s32[4,8,8,128]{3,1,2,0:T(8,128)S(1)} fusion(s32[1,1,32,1024]{3,2,1,0:T(8,128)} %param.12, s32[1,1,32,1024]{3,2,1,0:T(8,128)} %param.13), kind=kLoop, calls=%fused_computation | loop fusion | flops 65536 | bytes 393216
  1.8 0.0 copy-start
  1.8 1.4 %copy-done = bf16[1,1,32,25,1024]{4,2,3,1,0:T(8,128)(2,1)S(1)} copy-done((bf16[1,1,32,25,1024]{4,2,3,1,0:T(8,128)(2,1)S(1)}, bf16[1,1,32,25,1024]{4,2,3,1,0:T(8,128)(2,1)}, u32[]{:S(2)}) %copy-start) | copy-done | bytes 1638424
  3.2 1.0 %copy-done.1 = bf16[1,1,32,8,1024]{4,3,2,1,0:T(8,128)(2,1)S(1)} copy-done((bf16[1,1,32,8,1024]{4,3,2,1,0:T(8,128)(2,1)S(1)}, bf16[1,1,32,8,1024]{4,3,2,1,0:T(8,128)(2,1)}, u32[]{:S(2)}) %copy-start.1) | copy-done | bytes 524312
  4.3 0.7 copy-done.4
  4.9 31.5 %shard_map.121 = (bf16[1,1,25,32,1024]{4,3,2,1,0:T(8,128)(2,1)}, f32[32,8,128]{2,1,0:T(8,128)S(1)}) custom-call(s32[32]{0:T(128)S(1)} %bitcast.28, bf16[1,1,25,32,1024]{4,3,2,1,0:T(8,128)(2,1)S(1)} %bitcast.24, bf16[1,1,32,8,1024]{4,3,2,1,0:T(8,128)(2,1)S(1)} %copy-done.1, s32[32,8,128]{2,1,0:T(8,128)S(1)} %bitcast.25), custom_call_target="tpu_custom_call" | custom-call | tf_op jit(solution)/shard_map/pallas_call | solution.py:181
  36.4 0.3 reduce_sum.27
  36.7 0.0 copy-done.5
  36.7 0.0 copy-done.8
  36.8 0.1 select_reduce_fusion
  36.8 0.7 all_to_all.6
  37.5 18.9 %all-to-all-start = ((f32[4,1,16]{2,1,0:T(1,128)}), f32[4,1,16]{2,1,0:T(1,128)S(1)}, u32[]{:S(2)}, u32[]{:S(2)}) async-start(f32[4,1,16]{2,1,0:T(1,128)} %bitcast.6), calls=%async_computation | async-start | bytes 4096 | tf_op jit(solution)/shard_map/all_to_all | solution.py:214
  56.4 0.0 copy-done.6
  56.5 0.0 copy-done.7
  56.5 0.0 copy-done.2
  56.5 11.9 %shard_map.122 = (bf16[1,1,25,8,1024]{4,3,2,1,0:T(8,128)(2,1)}, f32[8,8,128]{2,1,0:T(8,128)}) custom-call(s32[8]{0:T(128)S(1)} %broadcast_1_dest_ref.2.dest_ref, bf16[1,1,25,8,1024]{4,3,2,1,0:T(8,128)(2,1)S(1)} %bitcast.26, bf16[1,1,8,8,1024]{4,3,2,1,0:T(8,128)(2,1)S(1)} %copy-done.3, s32[8,8,128]{2,1,0:T(8,128)S(1)} %bitcast.27), custom_call_target="tpu_custom_call" | custom-call | tf_op jit(solution)/shard_map/pallas_call | solution.py:181
  68.4 0.0 all-to-all-done
  68.4 0.5 reduce_sum.29
  (9 shorter events, 0.1 us)
Async XLA Ops:
  0.6 36.1 %copy-start.5 = (s32[1,1,32]{2,1,0:T(1,128)S(1)}, s32[1,1,32]{2,1,0:T(1,128)}, u32[]{:S(2)}) copy-start(s32[1,1,32]{2,1,0:T(1,128)} %param.14) | copy-start | bytes 388
  0.6 36.1 %copy-start.8 = (s32[1,1,32]{2,1,0:T(1,128)S(1)}, s32[1,1,32]{2,1,0:T(1,128)}, u32[]{:S(2)}) copy-start(s32[1,1,32]{2,1,0:T(1,128)} %param.15) | copy-start | bytes 388
  0.7 55.8 %copy-start.6 = (s32[1,1,8,1024]{3,2,1,0:T(8,128)S(1)}, s32[1,1,8,1024]{3,2,1,0:T(8,128)}, u32[]{:S(2)}) copy-start(s32[1,1,8,1024]{3,2,1,0:T(8,128)} %param.18) | copy-start | bytes 98308
  0.7 55.8 %copy-start.7 = (s32[1,1,8,1024]{3,2,1,0:T(8,128)S(1)}, s32[1,1,8,1024]{3,2,1,0:T(8,128)}, u32[]{:S(2)}) copy-start(s32[1,1,8,1024]{3,2,1,0:T(8,128)} %param.19) | copy-start | bytes 98308
  0.7 55.8 %copy-start.2 = (bf16[1,1,8,25,1024]{4,2,3,1,0:T(8,128)(2,1)S(1)}, bf16[1,1,8,25,1024]{4,2,3,1,0:T(8,128)(2,1)}, u32[]{:S(2)}) copy-start(bf16[1,1,8,25,1024]{4,2,3,1,0:T(8,128)(2,1)} %param.16) | copy-start | bytes 1228804
  0.7 55.8 %copy-start.3 = (bf16[1,1,8,8,1024]{4,3,2,1,0:T(8,128)(2,1)S(1)}, bf16[1,1,8,8,1024]{4,3,2,1,0:T(8,128)(2,1)}, u32[]{:S(2)}) copy-start(bf16[1,1,8,8,1024]{4,3,2,1,0:T(8,128)(2,1)} %u_ref.3) | copy-start | bytes 393220
  1.8 1.4 %copy-start = (bf16[1,1,32,25,1024]{4,2,3,1,0:T(8,128)(2,1)S(1)}, bf16[1,1,32,25,1024]{4,2,3,1,0:T(8,128)(2,1)}, u32[]{:S(2)}) copy-start(bf16[1,1,32,25,1024]{4,2,3,1,0:T(8,128)(2,1)} %param.10) | copy-start | bytes 4915204
  3.2 1.0 %copy-start.1 = (bf16[1,1,32,8,1024]{4,3,2,1,0:T(8,128)(2,1)S(1)}, bf16[1,1,32,8,1024]{4,3,2,1,0:T(8,128)(2,1)}, u32[]{:S(2)}) copy-start(bf16[1,1,32,8,1024]{4,3,2,1,0:T(8,128)(2,1)} %u_ref.2) | copy-start | bytes 1572868
  4.3 0.7 copy-start.4
  37.5 30.8 %all-to-all-start = ((f32[4,1,16]{2,1,0:T(1,128)}), f32[4,1,16]{2,1,0:T(1,128)S(1)}, u32[]{:S(2)}, u32[]{:S(2)}) async-start(f32[4,1,16]{2,1,0:T(1,128)} %bitcast.6), calls=%async_computation | async-start | bytes 4096 | tf_op jit(solution)/shard_map/all_to_all | solution.py:214
